TPU v7x, 256 devices: a whole 4x4x8 slice. The times are simulated.
256 devices in a mesh: gx: 8 (over y, core), gy: 8 (over z_hi, x), af: 4 (over z_lo).
Axes of the slice: x: 4, y: 4, z: 8 (z_hi: 2, z_lo: 4; z = z_hi * 4 + z_lo), core: 2. Of those that a mesh axis runs over, the one named last changes fastest.
Arguments:
- volume: bfloat16 [32, 32, 128, 128], P('af', 'gx', 'gy'), may hold values from -6 to 6
- weight_one: bfloat16 [32, 32, 3, 3, 3], P('af'), may hold values from -0.21875 to 0.21875
- bias_one: float32 [32], P('af'), may hold values from -1 to 1
- weight_two: bfloat16 [32, 32, 3, 3, 3], P('af'), may hold values from -0.21875 to 0.21875
- cotangent: bfloat16 [32, 32, 128, 128], P('af', 'gx', 'gy'), may hold values from -6 to 6
Outputs:
- output: bfloat16 [32, 32, 128, 128], P('af', 'gx', 'gy')
- input_grad: bfloat16 [32, 32, 128, 128], P('af', 'gx', 'gy')
- grad_one: float32 [32, 32, 3, 3, 3], P('af')
- bias_grad: float32 [32], P('af')
- grad_two: float32 [32, 32, 3, 3, 3], P('af')
All inputs are finite; a program needn't handle non-finite values.
Results may differ from a plain program's by a relative error of at most 0.0065.
Values may be sent and summed in bfloat16 or wider, within the bound.
A program may use at most 64 MiB of HBM per device.

v0:
```python
import math
import jax
import jax.numpy as jnp
from jax import lax
from jax.sharding import PartitionSpec as P


def with_halo(cells, sides, width):
    for axis, dim in sides:
        count = lax.axis_size(axis)
        ends = count - 1
        head = lax.slice_in_dim(cells, 0, width, axis=dim)
        tail = lax.slice_in_dim(cells, cells.shape[dim] - width, cells.shape[dim], axis=dim)
        cells = jnp.concatenate(
            [
                lax.ppermute(tail, axis, [(i, (i + 1) % count) for i in range(ends)]),
                cells,
                lax.ppermute(head, axis, [((i + 1) % count, i) for i in range(ends)]),
            ],
            axis=dim,
        )
    return cells


def conv_valid(padded, weight):
    size_x = padded.shape[1] - 2
    size_y = padded.shape[2] - 2
    size_z = padded.shape[3] - 2
    total = jnp.zeros((weight.shape[0], size_x, size_y, size_z), jnp.float32)
    for off_x in range(3):
        for off_y in range(3):
            for off_z in range(3):
                window = padded[
                    :, off_x : off_x + size_x, off_y : off_y + size_y, off_z : off_z + size_z
                ]
                total = total + jnp.einsum(
                    "oi,ixyz->oxyz",
                    weight[:, :, off_x, off_y, off_z],
                    window,
                    preferred_element_type=jnp.float32,
                )
    return total


def kernel_grad(padded, cot_field):
    size_x = cot_field.shape[1]
    size_y = cot_field.shape[2]
    size_z = cot_field.shape[3]
    blocks = []
    for off_x in range(3):
        for off_y in range(3):
            for off_z in range(3):
                window = padded[
                    :, off_x : off_x + size_x, off_y : off_y + size_y, off_z : off_z + size_z
                ]
                blocks.append(
                    jnp.einsum(
                        "oxyz,ixyz->oi", cot_field, window, preferred_element_type=jnp.float32
                    )
                )
    stacked = jnp.stack(blocks, axis=-1)
    return stacked.reshape(cot_field.shape[0], padded.shape[0], 3, 3, 3)


def flipped(weight):
    return jnp.transpose(jnp.flip(weight, (2, 3, 4)), (1, 0, 2, 3, 4))


def depth_pad(values):
    return jnp.pad(values, ((0, 0), (0, 0), (0, 0), (1, 1)))


def full_padded(values):
    gathered = lax.all_gather(values, "af", axis=0, tiled=True)
    rimmed = with_halo(gathered, (("gx", 1), ("gy", 2)), 1)
    return depth_pad(rimmed)


def silu_grad(hidden_grad, pre_act):
    sigma_vals = jax.nn.sigmoid(pre_act)
    return (hidden_grad * sigma_vals * (1.0 + pre_act * (1.0 - sigma_vals))).astype(jnp.bfloat16)


def body(volume, weight_one, bias_one, weight_two, cotangent):
    own_rows = volume.shape[0]
    vol_pad = full_padded(volume)
    pre_act = conv_valid(vol_pad, weight_one) + bias_one[:, None, None, None]
    hidden = jax.nn.silu(pre_act).astype(jnp.bfloat16)
    hid_pad = full_padded(hidden)
    output = conv_valid(hid_pad, weight_two).astype(jnp.bfloat16)
    local_two = kernel_grad(hid_pad, cotangent)
    every_one, every_two = (
        lax.all_gather(weight_one, "af", axis=0, tiled=True),
        lax.all_gather(weight_two, "af", axis=0, tiled=True),
    )
    first_row = lax.axis_index("af") * own_rows

    def transposed(cot_field, every_w):
        padded = full_padded(cot_field)
        turned = lax.dynamic_slice_in_dim(flipped(every_w), first_row, own_rows, 0)
        return conv_valid(padded, turned)

    hidden_grad = transposed(cotangent, every_two)
    pre_grad = silu_grad(hidden_grad, pre_act)
    local_one = kernel_grad(vol_pad, pre_grad)
    local_bias = jnp.sum(pre_grad, axis=(1, 2, 3), dtype=jnp.float32)
    input_grad = transposed(pre_grad, every_one).astype(jnp.bfloat16)
    summed_one, summed_bias, summed_two = lax.psum((local_one, local_bias, local_two), ("gx", "gy"))
    cell_total = (
        volume.shape[1]
        * lax.axis_size("gx")
        * volume.shape[2]
        * lax.axis_size("gy")
        * volume.shape[3]
    )
    grad_scale = 1.0 / math.sqrt(cell_total)
    return (
        output,
        input_grad,
        summed_one * grad_scale,
        summed_bias * grad_scale,
        summed_two * grad_scale,
    )


def solution(mesh):
    return jax.shard_map(
        body,
        mesh=mesh,
        in_specs=(
            P("af", "gx", "gy", None),
            P("af", None, None, None, None),
            P("af"),
            P("af", None, None, None, None),
            P("af", "gx", "gy", None),
        ),
        out_specs=(
            P("af", "gx", "gy", None),
            P("af", "gx", "gy", None),
            P("af", None, None, None, None),
            P("af"),
            P("af", None, None, None, None),
        ),
        check_vma=False,
    )
```

profile of v0, /device:TPU:0, one launch (start us, length us, event | category | flops | bytes accessed | tf_op | source)
XLA Modules:
  0.0 645.6 jit_solution(11498958030644135914)
XLA Ops:
  0.6 1.0 copy.43
  1.7 14.6 %all_gather.18 = bf16[32,4,16,128]{3,0,2,1:T(8,128)(2,1)S(1)} all-gather(bf16[8,4,16,128]{3,0,2,1:T(8,128)(2,1)S(1)} %copy.43), channel_id=1, replica_groups=mesh['gx'=8,'gy'=8,'af'=4] {'af'}, dimensions={0}, use_global_device_ids=true | all-gather | bytes 655360 | tf_op jit(solution)/shard_map/all_gather | solution.py:74
  16.3 1.3 collective-permute-start
  17.6 1.3 collective-permute-start.1
  19.9 15.3 %all_gather.22 = bf16[32,4,16,128]{3,0,2,1:T(8,128)(2,1)S(1)} all-gather(bf16[8,4,16,128]{3,0,2,1:T(8,128)(2,1)S(1)} %copy.46), channel_id=1, replica_groups=mesh['gx'=8,'gy'=8,'af'=4] {'af'}, dimensions={0}, use_global_device_ids=true | all-gather | bytes 655360 | tf_op jit(solution)/shard_map/all_gather | solution.py:74
  35.2 2.1 collective-permute-start.8
  37.4 1.3 collective-permute-start.9
  38.9 13.0 %all_gather.21 = bf16[32,32,3,3,3]{1,0,4,3,2:T(8,128)(2,1)S(1)} all-gather(bf16[8,32,3,3,3]{1,0,4,3,2:T(8,128)(2,1)S(1)} %copy-done.48), channel_id=1, replica_groups=mesh['gx'=8,'gy'=8,'af'=4] {'af'}, dimensions={0}, use_global_device_ids=true | all-gather | bytes 69120 | tf_op jit(solution)/shard_map/all_gather | solution.py:94
  52.3 13.0 %all_gather.20 = bf16[32,32,3,3,3]{1,0,4,3,2:T(8,128)(2,1)S(1)} all-gather(bf16[8,32,3,3,3]{1,0,4,3,2:T(8,128)(2,1)S(1)} %copy-done.50), channel_id=1, replica_groups=mesh['gx'=8,'gy'=8,'af'=4] {'af'}, dimensions={0}, use_global_device_ids=true | all-gather | bytes 69120 | tf_op jit(solution)/shard_map/all_gather | solution.py:93
  66.0 3.4 collective-permute-start.2
  69.4 1.3 collective-permute-start.3
  71.2 4.5 collective-permute-start.10
  75.8 1.5 collective-permute-start.11
  92.0 15.4 %all_gather.23 = bf16[32,4,16,128]{3,0,2,1:T(8,128)(2,1)S(1)} all-gather(bf16[8,4,16,128]{3,0,2,1:T(8,128)(2,1)S(1)} %get-tuple-element.51), channel_id=1, replica_groups=mesh['gx'=8,'gy'=8,'af'=4] {'af'}, dimensions={0}, use_global_device_ids=true | all-gather | bytes 655360 | tf_op jit(solution)/shard_map/all_gather | solution.py:74
  107.4 14.4 %all_gather.19 = bf16[32,4,16,128]{3,0,2,1:T(8,128)(2,1)S(1)} all-gather(bf16[8,4,16,128]{3,0,2,1:T(8,128)(2,1)S(1)} %get-tuple-element.48), channel_id=1, replica_groups=mesh['gx'=8,'gy'=8,'af'=4] {'af'}, dimensions={0}, use_global_device_ids=true | all-gather | bytes 655360 | tf_op jit(solution)/shard_map/all_gather | solution.py:74
  122.7 1.3 collective-permute-start.4
  123.9 1.5 collective-permute-start.5
  132.2 8.9 %collective-permute-start.12 = (bf16[32,1,16,128]{3,0,2,1:T(8,128)(2,1)S(1)}, bf16[32,1,16,128]{3,0,2,1:T(8,128)(2,1)S(1)}, u32[]{:S(2)}, u32[]{:S(2)}) collective-permute-start(bf16[32,1,16,128]{3,0,2,1:T(8,128)(2,1)S(1)} %get-tuple-element.27), channel_id=1, source_target_pairs={{0,32},{32,64},{64,96},{96,128},{128,160},{160,192},{192,224},{1,3... | collective-permute-start | bytes 393224 | tf_op jit(solution)/shard_map/ppermute | solution.py:16
  141.1 1.3 collective-permute-start.13
  144.3 4.4 collective-permute-start.6
  148.7 1.3 collective-permute-start.7
  150.2 9.7 %collective-permute-start.14 = (bf16[32,6,1,128]{3,0,2,1:T(8,128)(2,1)S(1)}, bf16[32,6,1,128]{3,0,2,1:T(8,128)(2,1)S(1)}, u32[]{:S(2)}, u32[]{:S(2)}) collective-permute-start(bf16[32,6,1,128]{3,0,2,1:T(8,128)(2,1)S(1)} %get-tuple-element.18), channel_id=1, source_target_pairs={{0,4},{4,8},{8,12},{12,16},{16,20},{20,24},{24,28},{1,5},{5,9},{9,... | collective-permute-start | bytes 147464 | tf_op jit(solution)/shard_map/ppermute | solution.py:16
  160.0 1.3 collective-permute-start.15
  164.8 7.0 %collective-permute-done.15 = bf16[32,6,1,128]{3,0,2,1:T(8,128)(2,1)S(1)} collective-permute-done((bf16[32,6,1,128]{3,0,2,1:T(8,128)(2,1)S(1)}, bf16[32,6,1,128]{3,0,2,1:T(8,128)(2,1)S(1)}, u32[]{:S(2)}, u32[]{:S(2)}) %collective-permute-start.15) | collective-permute-done | bytes 49184 | tf_op jit(solution)/shard_map/ppermute | solution.py:18
  173.7 1.0 fusion.228
  175.6 1.0 fusion.232
  177.5 1.0 fusion.236
  179.5 1.0 fusion.242
  181.4 1.0 fusion.209
  183.3 1.0 fusion.215
  185.3 1.0 fusion.221
  187.2 1.0 fusion.203
  190.3 1.0 fusion.310
  192.3 1.1 fusion.316
  194.2 1.0 fusion.322
  196.1 1.1 fusion.328
  198.1 1.1 convolution_bitcast_fusion.11
  200.0 1.0 convolution_bitcast_fusion.13
  201.1 1.0 convolution_bitcast_fusion.7
  203.0 1.1 convolution_bitcast_fusion.9
  213.4 413.0 %all-reduce.4 = (f32[8,32,3,3,3]{1,0,4,3,2:T(8,128)}, f32[8]{0:T(128)S(1)}, f32[8,32,3,3,3]{1,0,4,3,2:T(8,128)}) all-reduce(f32[8,32,3,3,3]{1,0,4,3,2:T(8,128)} %bitcast.1393, f32[8]{0:T(128)S(1)} %get-tuple-element.50, f32[8,32,3,3,3]{1,0,4,3,2:T(8,128)} %bitcast.1394), channel_id=1, replica_groups=mesh['gx'=8,'gy'=8,'af'=4] {'gx','gy'}, use_global_device_ids=true, to_apply=%region_0.1 | all-reduce | flops 13832 | bytes 110656 | tf_op jit(solution)/shard_map/psum | solution.py:108
  627.0 1.4 fusion.187
  628.3 1.2 fusion.181
  631.6 1.0 fusion.178
  634.5 1.1 fusion.108
  636.4 1.0 fusion.411
  640.3 1.0 fusion.391
  643.1 1.1 fusion.109
  (309 shorter events, 66.1 us)
Async XLA Ops:
  0.6 38.1 %copy-start.50 = (bf16[8,32,3,3,3]{1,0,4,3,2:T(8,128)(2,1)S(1)}, bf16[8,32,3,3,3]{1,0,4,3,2:T(8,128)(2,1)}, u32[]{:S(2)}) copy-start(bf16[8,32,3,3,3]{1,0,4,3,2:T(8,128)(2,1)} %param.6) | copy-start | bytes 41476
  1.7 37.2 %copy-start.48 = (bf16[8,32,3,3,3]{1,0,4,3,2:T(8,128)(2,1)S(1)}, bf16[8,32,3,3,3]{1,0,4,3,2:T(8,128)(2,1)}, u32[]{:S(2)}) copy-start(bf16[8,32,3,3,3]{1,0,4,3,2:T(8,128)(2,1)} %param.8) | copy-start | bytes 41476
  16.3 49.2 %collective-permute-start = (bf16[32,1,16,128]{3,0,2,1:T(8,128)(2,1)S(1)}, bf16[32,1,16,128]{3,0,2,1:T(8,128)(2,1)S(1)}, u32[]{:S(2)}, u32[]{:S(2)}) collective-permute-start(bf16[32,1,16,128]{3,0,2,1:T(8,128)(2,1)S(1)} %get-tuple-element.39), channel_id=1, source_target_pairs={{0,32},{32,64},{64,96},{96,128},{128,160},{160,192},{192,224},{1,3... | collective-permute-start | bytes 393224 | tf_op jit(solution)/shard_map/ppermute | solution.py:16
  17.6 48.3 %collective-permute-start.1 = (bf16[32,1,16,128]{3,0,2,1:T(8,128)(2,1)S(1)}, bf16[32,1,16,128]{3,0,2,1:T(8,128)(2,1)S(1)}, u32[]{:S(2)}, u32[]{:S(2)}) collective-permute-start(bf16[32,1,16,128]{3,0,2,1:T(8,128)(2,1)S(1)} %get-tuple-element.38), channel_id=1, source_target_pairs={{32,0},{64,32},{96,64},{128,96},{160,128},{192,160},{224,192},{33,... | collective-permute-start | bytes 393224 | tf_op jit(solution)/shard_map/ppermute | solution.py:18
  35.2 35.8 %collective-permute-start.8 = (bf16[32,1,16,128]{3,0,2,1:T(8,128)(2,1)S(1)}, bf16[32,1,16,128]{3,0,2,1:T(8,128)(2,1)S(1)}, u32[]{:S(2)}, u32[]{:S(2)}) collective-permute-start(bf16[32,1,16,128]{3,0,2,1:T(8,128)(2,1)S(1)} %get-tuple-element.29), channel_id=1, source_target_pairs={{0,32},{32,64},{64,96},{96,128},{128,160},{160,192},{192,224},{1,3... | collective-permute-start | bytes 393224 | tf_op jit(solution)/shard_map/ppermute | solution.py:16
  37.4 33.8 %collective-permute-start.9 = (bf16[32,1,16,128]{3,0,2,1:T(8,128)(2,1)S(1)}, bf16[32,1,16,128]{3,0,2,1:T(8,128)(2,1)S(1)}, u32[]{:S(2)}, u32[]{:S(2)}) collective-permute-start(bf16[32,1,16,128]{3,0,2,1:T(8,128)(2,1)S(1)} %get-tuple-element.28), channel_id=1, source_target_pairs={{32,0},{64,32},{96,64},{128,96},{160,128},{192,160},{224,192},{33,... | collective-permute-start | bytes 393224 | tf_op jit(solution)/shard_map/ppermute | solution.py:18
  65.5 121.7 %copy-start.47 = (bf16[8,32,3,3,3]{1,0,4,3,2:T(8,128)(2,1)}, bf16[8,32,3,3,3]{1,0,4,3,2:T(8,128)(2,1)S(1)}, u32[]{:S(2)}) copy-start(bf16[8,32,3,3,3]{1,0,4,3,2:T(8,128)(2,1)S(1)} %dynamic-slice_bitcast_fusion.1) | copy-start | bytes 41476
  66.0 11.6 %collective-permute-start.2 = (bf16[32,6,1,128]{3,0,2,1:T(8,128)(2,1)S(1)}, bf16[32,6,1,128]{3,0,2,1:T(8,128)(2,1)S(1)}, u32[]{:S(2)}, u32[]{:S(2)}) collective-permute-start(bf16[32,6,1,128]{3,0,2,1:T(8,128)(2,1)S(1)} %get-tuple-element.24), channel_id=1, source_target_pairs={{0,4},{4,8},{8,12},{12,16},{16,20},{20,24},{24,28},{1,5},{5,9},{9,... | collective-permute-start | bytes 147464 | tf_op jit(solution)/shard_map/ppermute | solution.py:16
  69.4 8.3 %collective-permute-start.3 = (bf16[32,6,1,128]{3,0,2,1:T(8,128)(2,1)S(1)}, bf16[32,6,1,128]{3,0,2,1:T(8,128)(2,1)S(1)}, u32[]{:S(2)}, u32[]{:S(2)}) collective-permute-start(bf16[32,6,1,128]{3,0,2,1:T(8,128)(2,1)S(1)} %get-tuple-element.25), channel_id=1, source_target_pairs={{4,0},{8,4},{12,8},{16,12},{20,16},{24,20},{28,24},{5,1},{9,5},{13... | collective-permute-start | bytes 147464 | tf_op jit(solution)/shard_map/ppermute | solution.py:18
  71.2 11.8 %collective-permute-start.10 = (bf16[32,6,1,128]{3,0,2,1:T(8,128)(2,1)S(1)}, bf16[32,6,1,128]{3,0,2,1:T(8,128)(2,1)S(1)}, u32[]{:S(2)}, u32[]{:S(2)}) collective-permute-start(bf16[32,6,1,128]{3,0,2,1:T(8,128)(2,1)S(1)} %get-tuple-element.20), channel_id=1, source_target_pairs={{0,4},{4,8},{8,12},{12,16},{16,20},{20,24},{24,28},{1,5},{5,9},{9,... | collective-permute-start | bytes 147464 | tf_op jit(solution)/shard_map/ppermute | solution.py:16
  75.8 7.3 %collective-permute-start.11 = (bf16[32,6,1,128]{3,0,2,1:T(8,128)(2,1)S(1)}, bf16[32,6,1,128]{3,0,2,1:T(8,128)(2,1)S(1)}, u32[]{:S(2)}, u32[]{:S(2)}) collective-permute-start(bf16[32,6,1,128]{3,0,2,1:T(8,128)(2,1)S(1)} %get-tuple-element.21), channel_id=1, source_target_pairs={{4,0},{8,4},{12,8},{16,12},{20,16},{24,20},{28,24},{5,1},{9,5},{13... | collective-permute-start | bytes 147464 | tf_op jit(solution)/shard_map/ppermute | solution.py:18
  122.7 21.2 %collective-permute-start.4 = (bf16[32,1,16,128]{3,0,2,1:T(8,128)(2,1)S(1)}, bf16[32,1,16,128]{3,0,2,1:T(8,128)(2,1)S(1)}, u32[]{:S(2)}, u32[]{:S(2)}) collective-permute-start(bf16[32,1,16,128]{3,0,2,1:T(8,128)(2,1)S(1)} %get-tuple-element.34), channel_id=1, source_target_pairs={{0,32},{32,64},{64,96},{96,128},{128,160},{160,192},{192,224},{1,3... | collective-permute-start | bytes 393224 | tf_op jit(solution)/shard_map/ppermute | solution.py:16
  123.9 20.3 %collective-permute-start.5 = (bf16[32,1,16,128]{3,0,2,1:T(8,128)(2,1)S(1)}, bf16[32,1,16,128]{3,0,2,1:T(8,128)(2,1)S(1)}, u32[]{:S(2)}, u32[]{:S(2)}) collective-permute-start(bf16[32,1,16,128]{3,0,2,1:T(8,128)(2,1)S(1)} %get-tuple-element.33), channel_id=1, source_target_pairs={{32,0},{64,32},{96,64},{128,96},{160,128},{192,160},{224,192},{33,... | collective-permute-start | bytes 393224 | tf_op jit(solution)/shard_map/ppermute | solution.py:18
  132.2 17.8 %collective-permute-start.12 = (bf16[32,1,16,128]{3,0,2,1:T(8,128)(2,1)S(1)}, bf16[32,1,16,128]{3,0,2,1:T(8,128)(2,1)S(1)}, u32[]{:S(2)}, u32[]{:S(2)}) collective-permute-start(bf16[32,1,16,128]{3,0,2,1:T(8,128)(2,1)S(1)} %get-tuple-element.27), channel_id=1, source_target_pairs={{0,32},{32,64},{64,96},{96,128},{128,160},{160,192},{192,224},{1,3... | collective-permute-start | bytes 393224 | tf_op jit(solution)/shard_map/ppermute | solution.py:16
  141.1 9.1 %collective-permute-start.13 = (bf16[32,1,16,128]{3,0,2,1:T(8,128)(2,1)S(1)}, bf16[32,1,16,128]{3,0,2,1:T(8,128)(2,1)S(1)}, u32[]{:S(2)}, u32[]{:S(2)}) collective-permute-start(bf16[32,1,16,128]{3,0,2,1:T(8,128)(2,1)S(1)} %get-tuple-element.26), channel_id=1, source_target_pairs={{32,0},{64,32},{96,64},{128,96},{160,128},{192,160},{224,192},{33,... | collective-permute-start | bytes 393224 | tf_op jit(solution)/shard_map/ppermute | solution.py:18
  143.8 6.3 copy-start.51
  144.3 67.9 %copy-start.3 = (bf16[32,6,16,128]{3,0,2,1:T(8,128)(2,1)}, bf16[32,6,16,128]{3,0,2,1:T(8,128)(2,1)S(1)}, u32[]{:S(2)}) copy-start(bf16[32,6,16,128]{3,0,2,1:T(8,128)(2,1)S(1)} %get-tuple-element.43) | copy-start | bytes 2359300
  144.3 43.9 %collective-permute-start.6 = (bf16[32,6,1,128]{3,0,2,1:T(8,128)(2,1)S(1)}, bf16[32,6,1,128]{3,0,2,1:T(8,128)(2,1)S(1)}, u32[]{:S(2)}, u32[]{:S(2)}) collective-permute-start(bf16[32,6,1,128]{3,0,2,1:T(8,128)(2,1)S(1)} %get-tuple-element.22), channel_id=1, source_target_pairs={{0,4},{4,8},{8,12},{12,16},{16,20},{20,24},{24,28},{1,5},{5,9},{9,... | collective-permute-start | bytes 147464 | tf_op jit(solution)/shard_map/ppermute | solution.py:16
  148.7 39.5 %collective-permute-start.7 = (bf16[32,6,1,128]{3,0,2,1:T(8,128)(2,1)S(1)}, bf16[32,6,1,128]{3,0,2,1:T(8,128)(2,1)S(1)}, u32[]{:S(2)}, u32[]{:S(2)}) collective-permute-start(bf16[32,6,1,128]{3,0,2,1:T(8,128)(2,1)S(1)} %get-tuple-element.23), channel_id=1, source_target_pairs={{4,0},{8,4},{12,8},{16,12},{20,16},{24,20},{28,24},{5,1},{9,5},{13... | collective-permute-start | bytes 147464 | tf_op jit(solution)/shard_map/ppermute | solution.py:18
  150.2 21.7 %copy-start = (bf16[32,6,16,128]{3,0,2,1:T(8,128)(2,1)}, bf16[32,6,16,128]{3,0,2,1:T(8,128)(2,1)S(1)}, u32[]{:S(2)}) copy-start(bf16[32,6,16,128]{3,0,2,1:T(8,128)(2,1)S(1)} %constant_dynamic-update-slice_fusion.17) | copy-start | bytes 2359300
  150.2 14.6 %collective-permute-start.14 = (bf16[32,6,1,128]{3,0,2,1:T(8,128)(2,1)S(1)}, bf16[32,6,1,128]{3,0,2,1:T(8,128)(2,1)S(1)}, u32[]{:S(2)}, u32[]{:S(2)}) collective-permute-start(bf16[32,6,1,128]{3,0,2,1:T(8,128)(2,1)S(1)} %get-tuple-element.18), channel_id=1, source_target_pairs={{0,4},{4,8},{8,12},{12,16},{16,20},{20,24},{24,28},{1,5},{5,9},{9,... | collective-permute-start | bytes 147464 | tf_op jit(solution)/shard_map/ppermute | solution.py:16
  160.0 11.9 %collective-permute-start.15 = (bf16[32,6,1,128]{3,0,2,1:T(8,128)(2,1)S(1)}, bf16[32,6,1,128]{3,0,2,1:T(8,128)(2,1)S(1)}, u32[]{:S(2)}, u32[]{:S(2)}) collective-permute-start(bf16[32,6,1,128]{3,0,2,1:T(8,128)(2,1)S(1)} %get-tuple-element.19), channel_id=1, source_target_pairs={{4,0},{8,4},{12,8},{16,12},{20,16},{24,20},{28,24},{5,1},{9,5},{13... | collective-permute-start | bytes 147464 | tf_op jit(solution)/shard_map/ppermute | solution.py:18
  164.8 9.9 %copy-start.43 = (bf16[32,6,1,128]{3,0,2,1:T(8,128)(2,1)}, bf16[32,6,1,128]{3,0,2,1:T(8,128)(2,1)S(1)}, u32[]{:S(2)}) copy-start(bf16[32,6,1,128]{3,0,2,1:T(8,128)(2,1)S(1)} %collective-permute-done.14) | copy-start | bytes 147460
  188.3 21.9 %copy-start.55 = (bf16[32,6,1,128]{3,0,2,1:T(8,128)(2,1)}, bf16[32,6,1,128]{3,0,2,1:T(8,128)(2,1)S(1)}, u32[]{:S(2)}) copy-start(bf16[32,6,1,128]{3,0,2,1:T(8,128)(2,1)S(1)} %collective-permute-done.6) | copy-start | bytes 147460
  188.3 23.9 %copy-start.57 = (bf16[32,6,1,128]{3,0,2,1:T(8,128)(2,1)}, bf16[32,6,1,128]{3,0,2,1:T(8,128)(2,1)S(1)}, u32[]{:S(2)}) copy-start(bf16[32,6,1,128]{3,0,2,1:T(8,128)(2,1)S(1)} %collective-permute-done.7) | copy-start | bytes 147460
  626.4 3.2 copy-start.1
  626.4 3.2 copy-start.44
  626.9 3.6 copy-start.24
  626.9 3.6 copy-start.34
  626.9 3.6 copy-start.35
  626.9 3.6 copy-start.36
  626.9 3.6 copy-start.37
  626.9 3.6 copy-start.38
  626.9 3.6 copy-start.39
  626.9 3.6 copy-start.40
  627.0 3.6 copy-start.41
  627.0 3.6 copy-start.42
  634.5 2.9 copy-start.58
  636.3 2.8 copy-start.23
  636.3 2.8 copy-start.25
  636.3 2.9 copy-start.26
  636.3 2.9 copy-start.27
  636.3 2.9 copy-start.28
  636.3 2.9 copy-start.29
  636.3 2.9 copy-start.30
  636.3 2.9 copy-start.31
  636.3 2.9 copy-start.32
  636.4 2.9 copy-start.33
  (28 other events, 66.5 us)
where the time goes:
time: 647 us; the launch traced here: 646 us
  blocking collectives  499 us (77%)
  matrix products  80.8 us (12%)
  starting transfers between devices  46.4 us (7%)
  waiting for transfers between devices  7.08 us (1%)
    psum x1, blocking collectives, body(): lax.psum((local_one, local_bias, local_two), ('gx', 'gy'))  413 us
    dot_general x108, matrix products, conv_valid(): jnp.einsum('oi,ixyz->oxyz', weight[:, :, off_x, off_y, off_z], window, pr...  65.3 us
    all_gather x4, blocking collectives, full_padded(): gathered = lax.all_gather(values, 'af', axis=0, tiled=True)  59.7 us
    ppermute x8, starting transfers between devices, with_halo(): lax.ppermute(tail, axis, [(i, (i + 1) % count) for i in range(ends)])  35.7 us
    dot_general x54, matrix products, kernel_grad(): jnp.einsum('oxyz,ixyz->oi', cot_field, window, preferred_element_type=jnp...  15.6 us
    all_gather x1, blocking collectives, body(): lax.all_gather(weight_one, 'af', axis=0, tiled=True)  13 us
    all_gather x1, blocking collectives, body(): lax.all_gather(weight_two, 'af', axis=0, tiled=True)  13 us
  transfers between devices with their start and end apart: 16, of which 1 were waited for; matrix products, arithmetic and copies ran while one was open for 6% of the time, Pallas kernels for 0%

commit v1 on v0

--- a/solution.py
+++ b/solution.py
@@ -105,7 +105,9 @@
     local_one = kernel_grad(vol_pad, pre_grad)
     local_bias = jnp.sum(pre_grad, axis=(1, 2, 3), dtype=jnp.float32)
     input_grad = transposed(pre_grad, every_one).astype(jnp.bfloat16)
-    summed_one, summed_bias, summed_two = lax.psum((local_one, local_bias, local_two), ("gx", "gy"))
+    summed_one, summed_bias, summed_two = lax.psum(
+        lax.psum((local_one, local_bias, local_two), "gy"), "gx"
+    )
     cell_total = (
         volume.shape[1]
         * lax.axis_size("gx")

time: 647 us -> 334 us (0.52)
  the two profiles are of different devices: /device:TPU:0 before, /device:TPU:4 now
where the time goes in v1:
time: 334 us; the launch traced here: 330 us
  blocking collectives  172 us (51%)
  matrix products  80.7 us (24%)
  starting transfers between devices  54.3 us (16%)
  waiting for transfers between devices  10.5 us (3%)
  local copies, waits for them, and re-layouts  5.88 us (2%)
  other arithmetic  4.83 us (1%)
    dot_general x108, matrix products, conv_valid(): jnp.einsum('oi,ixyz->oxyz', weight[:, :, off_x, off_y, off_z], window, pr...  65.2 us
    all_gather x4, blocking collectives, full_padded(): gathered = lax.all_gather(values, 'af', axis=0, tiled=True)  60.4 us
    psum x1, blocking collectives, body(): lax.psum((local_one, local_bias, local_two), 'gy')  57.7 us
    ppermute x8, starting transfers between devices, with_halo(): lax.ppermute(tail, axis, [(i, (i + 1) % count) for i in range(ends)])  39.9 us
    psum x1, blocking collectives, body(): lax.psum(lax.psum((local_one, local_bias, local_two), 'gy'), 'gx')  27.9 us
    dot_general x54, matrix products, kernel_grad(): jnp.einsum('oxyz,ixyz->oi', cot_field, window, preferred_element_type=jnp...  15.5 us
    ppermute x8, starting transfers between devices, with_halo(): lax.ppermute(head, axis, [((i + 1) % count, i) for i in range(ends)])  14.4 us
    all_gather x1, blocking collectives, body(): lax.all_gather(weight_one, 'af', axis=0, tiled=True)  13 us
  transfers between devices with their start and end apart: 16, of which 2 were waited for; matrix products, arithmetic and copies ran while one was open for 11% of the time, Pallas kernels for 0%

profile of v1, /device:TPU:4, one launch (start us, length us, event | category | flops | bytes accessed | tf_op | source)
XLA Modules:
  0.0 330.3 jit_solution(2568736568988316463)
XLA Ops:
  0.6 1.0 copy.43
  1.7 16.4 %all_gather.18 = bf16[32,4,16,128]{3,0,2,1:T(8,128)(2,1)S(1)} all-gather(bf16[8,4,16,128]{3,0,2,1:T(8,128)(2,1)S(1)} %copy.43), channel_id=1, replica_groups=mesh['gx'=8,'gy'=8,'af'=4] {'af'}, dimensions={0}, use_global_device_ids=true | all-gather | bytes 655360 | tf_op jit(solution)/shard_map/all_gather | solution.py:74
  18.1 1.3 collective-permute-start
  19.4 1.3 collective-permute-start.1
  21.7 15.3 %all_gather.22 = bf16[32,4,16,128]{3,0,2,1:T(8,128)(2,1)S(1)} all-gather(bf16[8,4,16,128]{3,0,2,1:T(8,128)(2,1)S(1)} %copy.46), channel_id=1, replica_groups=mesh['gx'=8,'gy'=8,'af'=4] {'af'}, dimensions={0}, use_global_device_ids=true | all-gather | bytes 655360 | tf_op jit(solution)/shard_map/all_gather | solution.py:74
  37.0 2.1 collective-permute-start.8
  39.1 1.3 collective-permute-start.9
  40.6 13.0 %all_gather.21 = bf16[32,32,3,3,3]{1,0,4,3,2:T(8,128)(2,1)S(1)} all-gather(bf16[8,32,3,3,3]{1,0,4,3,2:T(8,128)(2,1)S(1)} %copy-done.48), channel_id=1, replica_groups=mesh['gx'=8,'gy'=8,'af'=4] {'af'}, dimensions={0}, use_global_device_ids=true | all-gather | bytes 69120 | tf_op jit(solution)/shard_map/all_gather | solution.py:94
  54.0 13.0 %all_gather.20 = bf16[32,32,3,3,3]{1,0,4,3,2:T(8,128)(2,1)S(1)} all-gather(bf16[8,32,3,3,3]{1,0,4,3,2:T(8,128)(2,1)S(1)} %copy-done.50), channel_id=1, replica_groups=mesh['gx'=8,'gy'=8,'af'=4] {'af'}, dimensions={0}, use_global_device_ids=true | all-gather | bytes 69120 | tf_op jit(solution)/shard_map/all_gather | solution.py:93
  67.7 3.1 collective-permute-start.2
  70.9 2.7 collective-permute-start.3
  74.1 6.8 %collective-permute-start.10 = (bf16[32,6,1,128]{3,0,2,1:T(8,128)(2,1)S(1)}, bf16[32,6,1,128]{3,0,2,1:T(8,128)(2,1)S(1)}, u32[]{:S(2)}, u32[]{:S(2)}) collective-permute-start(bf16[32,6,1,128]{3,0,2,1:T(8,128)(2,1)S(1)} %get-tuple-element.23), channel_id=1, source_target_pairs={{0,4},{4,8},{8,12},{12,16},{16,20},{20,24},{24,28},{1,5},{5,9},{9,... | collective-permute-start | bytes 147464 | tf_op jit(solution)/shard_map/ppermute | solution.py:16
  81.0 2.2 collective-permute-start.11
  88.9 4.0 %collective-permute-done.11 = bf16[32,6,1,128]{3,0,2,1:T(8,128)(2,1)S(1)} collective-permute-done((bf16[32,6,1,128]{3,0,2,1:T(8,128)(2,1)S(1)}, bf16[32,6,1,128]{3,0,2,1:T(8,128)(2,1)S(1)}, u32[]{:S(2)}, u32[]{:S(2)}) %collective-permute-start.11) | collective-permute-done | bytes 49184 | tf_op jit(solution)/shard_map/ppermute | solution.py:18
  101.9 14.2 %all_gather.23 = bf16[32,4,16,128]{3,0,2,1:T(8,128)(2,1)S(1)} all-gather(bf16[8,4,16,128]{3,0,2,1:T(8,128)(2,1)S(1)} %get-tuple-element.54), channel_id=1, replica_groups=mesh['gx'=8,'gy'=8,'af'=4] {'af'}, dimensions={0}, use_global_device_ids=true | all-gather | bytes 655360 | tf_op jit(solution)/shard_map/all_gather | solution.py:74
  116.1 14.5 %all_gather.19 = bf16[32,4,16,128]{3,0,2,1:T(8,128)(2,1)S(1)} all-gather(bf16[8,4,16,128]{3,0,2,1:T(8,128)(2,1)S(1)} %get-tuple-element.51), channel_id=1, replica_groups=mesh['gx'=8,'gy'=8,'af'=4] {'af'}, dimensions={0}, use_global_device_ids=true | all-gather | bytes 655360 | tf_op jit(solution)/shard_map/all_gather | solution.py:74
  131.5 1.3 collective-permute-start.4
  132.8 1.8 collective-permute-start.5
  141.3 8.5 %collective-permute-start.12 = (bf16[32,1,16,128]{3,0,2,1:T(8,128)(2,1)S(1)}, bf16[32,1,16,128]{3,0,2,1:T(8,128)(2,1)S(1)}, u32[]{:S(2)}, u32[]{:S(2)}) collective-permute-start(bf16[32,1,16,128]{3,0,2,1:T(8,128)(2,1)S(1)} %get-tuple-element.30), channel_id=1, source_target_pairs={{0,32},{32,64},{64,96},{96,128},{128,160},{160,192},{192,224},{1,3... | collective-permute-start | bytes 393224 | tf_op jit(solution)/shard_map/ppermute | solution.py:16
  149.8 1.3 collective-permute-start.13
  153.0 9.9 %collective-permute-start.6 = (bf16[32,6,1,128]{3,0,2,1:T(8,128)(2,1)S(1)}, bf16[32,6,1,128]{3,0,2,1:T(8,128)(2,1)S(1)}, u32[]{:S(2)}, u32[]{:S(2)}) collective-permute-start(bf16[32,6,1,128]{3,0,2,1:T(8,128)(2,1)S(1)} %get-tuple-element.25), channel_id=1, source_target_pairs={{0,4},{4,8},{8,12},{12,16},{16,20},{20,24},{24,28},{1,5},{5,9},{9,... | collective-permute-start | bytes 147464 | tf_op jit(solution)/shard_map/ppermute | solution.py:16
  162.9 1.9 collective-permute-start.7
  165.0 6.9 %collective-permute-start.14 = (bf16[32,6,1,128]{3,0,2,1:T(8,128)(2,1)S(1)}, bf16[32,6,1,128]{3,0,2,1:T(8,128)(2,1)S(1)}, u32[]{:S(2)}, u32[]{:S(2)}) collective-permute-start(bf16[32,6,1,128]{3,0,2,1:T(8,128)(2,1)S(1)} %get-tuple-element.21), channel_id=1, source_target_pairs={{0,4},{4,8},{8,12},{12,16},{16,20},{20,24},{24,28},{1,5},{5,9},{9,... | collective-permute-start | bytes 147464 | tf_op jit(solution)/shard_map/ppermute | solution.py:16
  171.9 1.9 collective-permute-start.15
  177.5 6.5 %collective-permute-done.15 = bf16[32,6,1,128]{3,0,2,1:T(8,128)(2,1)S(1)} collective-permute-done((bf16[32,6,1,128]{3,0,2,1:T(8,128)(2,1)S(1)}, bf16[32,6,1,128]{3,0,2,1:T(8,128)(2,1)S(1)}, u32[]{:S(2)}, u32[]{:S(2)}) %collective-permute-start.15) | collective-permute-done | bytes 49184 | tf_op jit(solution)/shard_map/ppermute | solution.py:18
  185.7 1.0 fusion.228
  187.7 1.0 fusion.232
  189.6 1.0 fusion.236
  191.5 1.0 fusion.242
  193.5 1.1 fusion.209
  195.4 1.0 fusion.215
  197.3 1.0 fusion.221
  199.2 1.0 fusion.203
  202.4 1.1 fusion.310
  204.3 1.0 fusion.316
  206.2 1.0 fusion.322
  208.1 1.1 fusion.328
  210.1 1.0 convolution_bitcast_fusion.11
  212.1 1.0 convolution_bitcast_fusion.13
  213.1 1.0 convolution_bitcast_fusion.7
  215.0 1.1 convolution_bitcast_fusion.9
  225.4 57.7 %all-reduce.4 = (f32[8,32,3,3,3]{1,0,4,3,2:T(8,128)}, f32[8]{0:T(128)S(1)}, f32[8,32,3,3,3]{1,0,4,3,2:T(8,128)}) all-reduce(f32[8,32,3,3,3]{1,0,4,3,2:T(8,128)} %bitcast.1393, f32[8]{0:T(128)S(1)} %get-tuple-element.53, f32[8,32,3,3,3]{1,0,4,3,2:T(8,128)} %bitcast.1394), channel_id=1, replica_groups=mesh['gx'=8,'gy'=8,'af'=4] {'gy'}, use_global_device_ids=true, to_apply=%region_0.1 | all-reduce | flops 13832 | bytes 110656 | tf_op jit(solution)/shard_map/psum | solution.py:109
  283.1 27.9 %all-reduce.5 = (f32[8,32,3,3,3]{1,0,4,3,2:T(8,128)}, f32[8]{0:T(128)S(1)}, f32[8,32,3,3,3]{1,0,4,3,2:T(8,128)}) all-reduce(f32[8,32,3,3,3]{1,0,4,3,2:T(8,128)} %get-tuple-element.15, f32[8]{0:T(128)S(1)} %get-tuple-element.16, f32[8,32,3,3,3]{1,0,4,3,2:T(8,128)} %get-tuple-element.17), channel_id=1, replica_groups=mesh['gx'=8,'gy'=8,'af'=4] {'gx'}, use_global_device_ids=true, to_apply=%region_1.2 | all-reduce | flops 13832 | bytes 110656 | tf_op jit(solution)/shard_map/psum | solution.py:108
  311.6 1.4 fusion.187
  312.9 1.2 fusion.181
  319.1 1.1 fusion.108
  320.9 1.0 fusion.411
  327.7 1.1 fusion.109
  (310 shorter events, 68.0 us)
Async XLA Ops:
  0.6 39.8 %copy-start.50 = (bf16[8,32,3,3,3]{1,0,4,3,2:T(8,128)(2,1)S(1)}, bf16[8,32,3,3,3]{1,0,4,3,2:T(8,128)(2,1)}, u32[]{:S(2)}) copy-start(bf16[8,32,3,3,3]{1,0,4,3,2:T(8,128)(2,1)} %param.6) | copy-start | bytes 41476
  1.7 39.0 %copy-start.48 = (bf16[8,32,3,3,3]{1,0,4,3,2:T(8,128)(2,1)S(1)}, bf16[8,32,3,3,3]{1,0,4,3,2:T(8,128)(2,1)}, u32[]{:S(2)}) copy-start(bf16[8,32,3,3,3]{1,0,4,3,2:T(8,128)(2,1)} %param.8) | copy-start | bytes 41476
  18.1 49.2 %collective-permute-start = (bf16[32,1,16,128]{3,0,2,1:T(8,128)(2,1)S(1)}, bf16[32,1,16,128]{3,0,2,1:T(8,128)(2,1)S(1)}, u32[]{:S(2)}, u32[]{:S(2)}) collective-permute-start(bf16[32,1,16,128]{3,0,2,1:T(8,128)(2,1)S(1)} %get-tuple-element.42), channel_id=1, source_target_pairs={{0,32},{32,64},{64,96},{96,128},{128,160},{160,192},{192,224},{1,3... | collective-permute-start | bytes 393224 | tf_op jit(solution)/shard_map/ppermute | solution.py:16
  19.4 48.3 %collective-permute-start.1 = (bf16[32,1,16,128]{3,0,2,1:T(8,128)(2,1)S(1)}, bf16[32,1,16,128]{3,0,2,1:T(8,128)(2,1)S(1)}, u32[]{:S(2)}, u32[]{:S(2)}) collective-permute-start(bf16[32,1,16,128]{3,0,2,1:T(8,128)(2,1)S(1)} %get-tuple-element.41), channel_id=1, source_target_pairs={{32,0},{64,32},{96,64},{128,96},{160,128},{192,160},{224,192},{33,... | collective-permute-start | bytes 393224 | tf_op jit(solution)/shard_map/ppermute | solution.py:18
  37.0 37.0 %collective-permute-start.8 = (bf16[32,1,16,128]{3,0,2,1:T(8,128)(2,1)S(1)}, bf16[32,1,16,128]{3,0,2,1:T(8,128)(2,1)S(1)}, u32[]{:S(2)}, u32[]{:S(2)}) collective-permute-start(bf16[32,1,16,128]{3,0,2,1:T(8,128)(2,1)S(1)} %get-tuple-element.32), channel_id=1, source_target_pairs={{0,32},{32,64},{64,96},{96,128},{128,160},{160,192},{192,224},{1,3... | collective-permute-start | bytes 393224 | tf_op jit(solution)/shard_map/ppermute | solution.py:16
  39.1 34.9 %collective-permute-start.9 = (bf16[32,1,16,128]{3,0,2,1:T(8,128)(2,1)S(1)}, bf16[32,1,16,128]{3,0,2,1:T(8,128)(2,1)S(1)}, u32[]{:S(2)}, u32[]{:S(2)}) collective-permute-start(bf16[32,1,16,128]{3,0,2,1:T(8,128)(2,1)S(1)} %get-tuple-element.31), channel_id=1, source_target_pairs={{32,0},{64,32},{96,64},{128,96},{160,128},{192,160},{224,192},{33,... | collective-permute-start | bytes 393224 | tf_op jit(solution)/shard_map/ppermute | solution.py:18
  67.3 132.0 %copy-start.47 = (bf16[8,32,3,3,3]{1,0,4,3,2:T(8,128)(2,1)}, bf16[8,32,3,3,3]{1,0,4,3,2:T(8,128)(2,1)S(1)}, u32[]{:S(2)}) copy-start(bf16[8,32,3,3,3]{1,0,4,3,2:T(8,128)(2,1)S(1)} %dynamic-slice_bitcast_fusion.1) | copy-start | bytes 41476
  67.7 15.8 %collective-permute-start.2 = (bf16[32,6,1,128]{3,0,2,1:T(8,128)(2,1)S(1)}, bf16[32,6,1,128]{3,0,2,1:T(8,128)(2,1)S(1)}, u32[]{:S(2)}, u32[]{:S(2)}) collective-permute-start(bf16[32,6,1,128]{3,0,2,1:T(8,128)(2,1)S(1)} %get-tuple-element.27), channel_id=1, source_target_pairs={{0,4},{4,8},{8,12},{12,16},{16,20},{20,24},{24,28},{1,5},{5,9},{9,... | collective-permute-start | bytes 147464 | tf_op jit(solution)/shard_map/ppermute | solution.py:16
  70.9 12.7 %collective-permute-start.3 = (bf16[32,6,1,128]{3,0,2,1:T(8,128)(2,1)S(1)}, bf16[32,6,1,128]{3,0,2,1:T(8,128)(2,1)S(1)}, u32[]{:S(2)}, u32[]{:S(2)}) collective-permute-start(bf16[32,6,1,128]{3,0,2,1:T(8,128)(2,1)S(1)} %get-tuple-element.28), channel_id=1, source_target_pairs={{4,0},{8,4},{12,8},{16,12},{20,16},{24,20},{28,24},{5,1},{9,5},{13... | collective-permute-start | bytes 147464 | tf_op jit(solution)/shard_map/ppermute | solution.py:18
  74.1 14.8 %collective-permute-start.10 = (bf16[32,6,1,128]{3,0,2,1:T(8,128)(2,1)S(1)}, bf16[32,6,1,128]{3,0,2,1:T(8,128)(2,1)S(1)}, u32[]{:S(2)}, u32[]{:S(2)}) collective-permute-start(bf16[32,6,1,128]{3,0,2,1:T(8,128)(2,1)S(1)} %get-tuple-element.23), channel_id=1, source_target_pairs={{0,4},{4,8},{8,12},{12,16},{16,20},{20,24},{24,28},{1,5},{5,9},{9,... | collective-permute-start | bytes 147464 | tf_op jit(solution)/shard_map/ppermute | solution.py:16
  81.0 12.0 %collective-permute-start.11 = (bf16[32,6,1,128]{3,0,2,1:T(8,128)(2,1)S(1)}, bf16[32,6,1,128]{3,0,2,1:T(8,128)(2,1)S(1)}, u32[]{:S(2)}, u32[]{:S(2)}) collective-permute-start(bf16[32,6,1,128]{3,0,2,1:T(8,128)(2,1)S(1)} %get-tuple-element.24), channel_id=1, source_target_pairs={{4,0},{8,4},{12,8},{16,12},{20,16},{24,20},{28,24},{5,1},{9,5},{13... | collective-permute-start | bytes 147464 | tf_op jit(solution)/shard_map/ppermute | solution.py:18
  131.5 21.0 %collective-permute-start.4 = (bf16[32,1,16,128]{3,0,2,1:T(8,128)(2,1)S(1)}, bf16[32,1,16,128]{3,0,2,1:T(8,128)(2,1)S(1)}, u32[]{:S(2)}, u32[]{:S(2)}) collective-permute-start(bf16[32,1,16,128]{3,0,2,1:T(8,128)(2,1)S(1)} %get-tuple-element.37), channel_id=1, source_target_pairs={{0,32},{32,64},{64,96},{96,128},{128,160},{160,192},{192,224},{1,3... | collective-permute-start | bytes 393224 | tf_op jit(solution)/shard_map/ppermute | solution.py:16
  132.8 20.1 %collective-permute-start.5 = (bf16[32,1,16,128]{3,0,2,1:T(8,128)(2,1)S(1)}, bf16[32,1,16,128]{3,0,2,1:T(8,128)(2,1)S(1)}, u32[]{:S(2)}, u32[]{:S(2)}) collective-permute-start(bf16[32,1,16,128]{3,0,2,1:T(8,128)(2,1)S(1)} %get-tuple-element.36), channel_id=1, source_target_pairs={{32,0},{64,32},{96,64},{128,96},{160,128},{192,160},{224,192},{33,... | collective-permute-start | bytes 393224 | tf_op jit(solution)/shard_map/ppermute | solution.py:18
  141.3 23.5 %collective-permute-start.12 = (bf16[32,1,16,128]{3,0,2,1:T(8,128)(2,1)S(1)}, bf16[32,1,16,128]{3,0,2,1:T(8,128)(2,1)S(1)}, u32[]{:S(2)}, u32[]{:S(2)}) collective-permute-start(bf16[32,1,16,128]{3,0,2,1:T(8,128)(2,1)S(1)} %get-tuple-element.30), channel_id=1, source_target_pairs={{0,32},{32,64},{64,96},{96,128},{128,160},{160,192},{192,224},{1,3... | collective-permute-start | bytes 393224 | tf_op jit(solution)/shard_map/ppermute | solution.py:16
  149.8 15.1 %collective-permute-start.13 = (bf16[32,1,16,128]{3,0,2,1:T(8,128)(2,1)S(1)}, bf16[32,1,16,128]{3,0,2,1:T(8,128)(2,1)S(1)}, u32[]{:S(2)}, u32[]{:S(2)}) collective-permute-start(bf16[32,1,16,128]{3,0,2,1:T(8,128)(2,1)S(1)} %get-tuple-element.29), channel_id=1, source_target_pairs={{32,0},{64,32},{96,64},{128,96},{160,128},{192,160},{224,192},{33,... | collective-permute-start | bytes 393224 | tf_op jit(solution)/shard_map/ppermute | solution.py:18
  152.5 12.4 %copy-start.51 = (f32[8,32,27]{1,0,2:T(8,128)}, f32[8,32,27]{1,0,2:T(8,128)S(1)}, u32[]{:S(2)}) copy-start(f32[8,32,27]{1,0,2:T(8,128)S(1)} %fusion.138) | copy-start | bytes 82948
  153.0 71.1 %copy-start.3 = (bf16[32,6,16,128]{3,0,2,1:T(8,128)(2,1)}, bf16[32,6,16,128]{3,0,2,1:T(8,128)(2,1)S(1)}, u32[]{:S(2)}) copy-start(bf16[32,6,16,128]{3,0,2,1:T(8,128)(2,1)S(1)} %get-tuple-element.46) | copy-start | bytes 2359300
  153.0 47.3 %collective-permute-start.6 = (bf16[32,6,1,128]{3,0,2,1:T(8,128)(2,1)S(1)}, bf16[32,6,1,128]{3,0,2,1:T(8,128)(2,1)S(1)}, u32[]{:S(2)}, u32[]{:S(2)}) collective-permute-start(bf16[32,6,1,128]{3,0,2,1:T(8,128)(2,1)S(1)} %get-tuple-element.25), channel_id=1, source_target_pairs={{0,4},{4,8},{8,12},{12,16},{16,20},{20,24},{24,28},{1,5},{5,9},{9,... | collective-permute-start | bytes 147464 | tf_op jit(solution)/shard_map/ppermute | solution.py:16
  162.9 37.4 %collective-permute-start.7 = (bf16[32,6,1,128]{3,0,2,1:T(8,128)(2,1)S(1)}, bf16[32,6,1,128]{3,0,2,1:T(8,128)(2,1)S(1)}, u32[]{:S(2)}, u32[]{:S(2)}) collective-permute-start(bf16[32,6,1,128]{3,0,2,1:T(8,128)(2,1)S(1)} %get-tuple-element.26), channel_id=1, source_target_pairs={{4,0},{8,4},{12,8},{16,12},{20,16},{24,20},{28,24},{5,1},{9,5},{13... | collective-permute-start | bytes 147464 | tf_op jit(solution)/shard_map/ppermute | solution.py:18
  165.0 19.0 %copy-start = (bf16[32,6,16,128]{3,0,2,1:T(8,128)(2,1)}, bf16[32,6,16,128]{3,0,2,1:T(8,128)(2,1)S(1)}, u32[]{:S(2)}) copy-start(bf16[32,6,16,128]{3,0,2,1:T(8,128)(2,1)S(1)} %constant_dynamic-update-slice_fusion.17) | copy-start | bytes 2359300
  165.0 12.5 %collective-permute-start.14 = (bf16[32,6,1,128]{3,0,2,1:T(8,128)(2,1)S(1)}, bf16[32,6,1,128]{3,0,2,1:T(8,128)(2,1)S(1)}, u32[]{:S(2)}, u32[]{:S(2)}) collective-permute-start(bf16[32,6,1,128]{3,0,2,1:T(8,128)(2,1)S(1)} %get-tuple-element.21), channel_id=1, source_target_pairs={{0,4},{4,8},{8,12},{12,16},{16,20},{20,24},{24,28},{1,5},{5,9},{9,... | collective-permute-start | bytes 147464 | tf_op jit(solution)/shard_map/ppermute | solution.py:16
  171.9 12.0 %collective-permute-start.15 = (bf16[32,6,1,128]{3,0,2,1:T(8,128)(2,1)S(1)}, bf16[32,6,1,128]{3,0,2,1:T(8,128)(2,1)S(1)}, u32[]{:S(2)}, u32[]{:S(2)}) collective-permute-start(bf16[32,6,1,128]{3,0,2,1:T(8,128)(2,1)S(1)} %get-tuple-element.22), channel_id=1, source_target_pairs={{4,0},{8,4},{12,8},{16,12},{20,16},{24,20},{28,24},{5,1},{9,5},{13... | collective-permute-start | bytes 147464 | tf_op jit(solution)/shard_map/ppermute | solution.py:18
  177.5 9.3 %copy-start.43 = (bf16[32,6,1,128]{3,0,2,1:T(8,128)(2,1)}, bf16[32,6,1,128]{3,0,2,1:T(8,128)(2,1)S(1)}, u32[]{:S(2)}) copy-start(bf16[32,6,1,128]{3,0,2,1:T(8,128)(2,1)S(1)} %collective-permute-done.14) | copy-start | bytes 147460
  183.9 2.9 copy-start.45
  200.3 21.9 %copy-start.55 = (bf16[32,6,1,128]{3,0,2,1:T(8,128)(2,1)}, bf16[32,6,1,128]{3,0,2,1:T(8,128)(2,1)S(1)}, u32[]{:S(2)}) copy-start(bf16[32,6,1,128]{3,0,2,1:T(8,128)(2,1)S(1)} %collective-permute-done.6) | copy-start | bytes 147460
  200.3 23.8 %copy-start.57 = (bf16[32,6,1,128]{3,0,2,1:T(8,128)(2,1)}, bf16[32,6,1,128]{3,0,2,1:T(8,128)(2,1)S(1)}, u32[]{:S(2)}) copy-start(bf16[32,6,1,128]{3,0,2,1:T(8,128)(2,1)S(1)} %collective-permute-done.7) | copy-start | bytes 147460
  311.0 3.2 copy-start.1
  311.0 3.2 copy-start.44
  311.5 3.6 %copy-start.24 = (f32[8,4,16,128]{3,0,2,1:T(8,128)S(1)}, f32[8,4,16,128]{3,0,2,1:T(8,128)}, u32[]{:S(2)}) copy-start(f32[8,4,16,128]{3,0,2,1:T(8,128)} %fusion.379) | copy-start | bytes 786436
  311.5 3.6 %copy-start.34 = (f32[8,4,16,128]{3,0,2,1:T(8,128)S(1)}, f32[8,4,16,128]{3,0,2,1:T(8,128)}, u32[]{:S(2)}) copy-start(f32[8,4,16,128]{3,0,2,1:T(8,128)} %fusion.238) | copy-start | bytes 786436
  311.5 3.6 %copy-start.35 = (f32[8,4,16,128]{3,0,2,1:T(8,128)S(1)}, f32[8,4,16,128]{3,0,2,1:T(8,128)}, u32[]{:S(2)}) copy-start(f32[8,4,16,128]{3,0,2,1:T(8,128)} %fusion.226) | copy-start | bytes 786436
  311.5 3.6 %copy-start.36 = (f32[8,4,16,128]{3,0,2,1:T(8,128)S(1)}, f32[8,4,16,128]{3,0,2,1:T(8,128)}, u32[]{:S(2)}) copy-start(f32[8,4,16,128]{3,0,2,1:T(8,128)} %fusion.228) | copy-start | bytes 786436
  311.5 3.6 %copy-start.37 = (f32[8,4,16,128]{3,0,2,1:T(8,128)S(1)}, f32[8,4,16,128]{3,0,2,1:T(8,128)}, u32[]{:S(2)}) copy-start(f32[8,4,16,128]{3,0,2,1:T(8,128)} %fusion.230) | copy-start | bytes 786436
  311.5 3.6 %copy-start.38 = (f32[8,4,16,128]{3,0,2,1:T(8,128)S(1)}, f32[8,4,16,128]{3,0,2,1:T(8,128)}, u32[]{:S(2)}) copy-start(f32[8,4,16,128]{3,0,2,1:T(8,128)} %fusion.232) | copy-start | bytes 786436
  311.5 3.6 %copy-start.39 = (f32[8,4,16,128]{3,0,2,1:T(8,128)S(1)}, f32[8,4,16,128]{3,0,2,1:T(8,128)}, u32[]{:S(2)}) copy-start(f32[8,4,16,128]{3,0,2,1:T(8,128)} %fusion.234) | copy-start | bytes 786436
  311.5 3.6 %copy-start.40 = (f32[8,4,16,128]{3,0,2,1:T(8,128)S(1)}, f32[8,4,16,128]{3,0,2,1:T(8,128)}, u32[]{:S(2)}) copy-start(f32[8,4,16,128]{3,0,2,1:T(8,128)} %fusion.236) | copy-start | bytes 786436
  311.5 3.6 %copy-start.41 = (f32[8,4,16,128]{3,0,2,1:T(8,128)S(1)}, f32[8,4,16,128]{3,0,2,1:T(8,128)}, u32[]{:S(2)}) copy-start(f32[8,4,16,128]{3,0,2,1:T(8,128)} %fusion.240) | copy-start | bytes 786436
  311.5 3.6 %copy-start.42 = (f32[8,4,16,128]{3,0,2,1:T(8,128)S(1)}, f32[8,4,16,128]{3,0,2,1:T(8,128)}, u32[]{:S(2)}) copy-start(f32[8,4,16,128]{3,0,2,1:T(8,128)} %fusion.242) | copy-start | bytes 786436
  319.1 2.9 copy-start.58
  320.9 2.8 copy-start.25
  320.9 2.8 copy-start.26
  320.9 2.8 copy-start.27
  320.9 2.8 copy-start.28
  320.9 2.8 copy-start.29
  320.9 2.8 copy-start.30
  320.9 2.8 copy-start.31
  320.9 2.8 copy-start.32
  320.9 2.8 copy-start.33
  (28 other events, 66.5 us)
